TPU v7x, 256 devices: a whole 4x4x8 slice. The times are simulated.
256 devices in a mesh: prow: 32 (over x, z), pcol: 8 (over y, core).
Axes of the slice: x: 4, y: 4, z: 8, core: 2. Of those that a mesh axis runs over, the one named last changes fastest.
Arguments:
- matrix: float32 [24, 512, 3, 4096], P(None, 'prow', None, 'pcol'), may hold values from -6 to 6
- pivots: int32 [2, 512], replicated, may hold values from 0 to 12287, as said below
- lower_inv: float32 [2, 512, 512], replicated
- upper_inv: float32 [2, 512, 512], replicated
Outputs:
- factored: float32 [24, 512, 3, 4096], P(None, 'prow', None, 'pcol')
Inputs may be any that keep to these rules, and one draw needn't show every extreme that they name: pivots[k, i] is at least k * 512 + i; every panel has one entry equal to 12287, and the first panel's first row keeps its place.
All inputs are finite; a program needn't handle non-finite values.
Results may differ from a plain program's by a relative error of at most 0.00011.
Values sent between devices are 32-bit elements; how exact they have to be, the bound alone decides.
A program may use at most 64 MiB of HBM per device.

v0:
```python
import functools

import jax
import jax.numpy as jnp
from jax import lax
from jax.experimental import pallas as pl
from jax.experimental.pallas import tpu as pltpu
from jax.sharding import Mesh
from jax.sharding import PartitionSpec as P

PROW = ("x", "z")
MESH = pl.DeviceIdType.MESH
NX, NZ = 4, 8


def in_order(parts, dim):
    shape = list(parts.shape[1:])
    shape[dim] *= parts.shape[0]
    return jnp.moveaxis(parts, 0, dim).reshape(shape)


def all_blocks(x, axes, order):
    parts = x
    for k in order:
        parts = lax.all_gather(parts, axes[k])
    done = order[::-1]
    back = [done.index(k) for k in range(len(axes))]
    parts = parts.transpose(*back, *range(len(axes), parts.ndim))
    return parts.reshape(-1, *x.shape)


def gathered_by_axis(x, axes, order, dim):
    return in_order(all_blocks(x, axes, order), dim)


def sum_by_axis(x, axes, dim):
    for axis in axes:
        x = lax.psum_scatter(x, axis, scatter_dimension=dim, tiled=True)
    return x


def broadcast(x, axis, root):
    return lax.dynamic_index_in_dim(lax.all_gather(x, axis), root, 0, keepdims=False)


def permutation(pivot_row, offset, panel_width, full_order):
    steps = jnp.arange(panel_width, dtype=jnp.int32)
    anchors = offset + steps
    earlier = steps[None, :] < steps[:, None]
    hits_anchor = (pivot_row[None, :] == anchors[:, None]) & earlier
    chain_from = jnp.max(jnp.where(hits_anchor, steps[None, :], -1), axis=1)
    pointer = jnp.where(chain_from >= 0, chain_from, steps)
    for level in range(max(1, panel_width.bit_length())):
        pointer = pointer[pointer]
    before_value = offset + pointer
    same_target = (pivot_row[None, :] == pivot_row[:, None]) & earlier
    last_before = jnp.max(jnp.where(same_target, steps[None, :], -1), axis=1)
    anchor_value = jnp.where(
        last_before >= 0, before_value[jnp.clip(last_before, 0, panel_width - 1)], pivot_row
    )
    later = steps[None, :] > steps[:, None]
    has_later = jnp.any((pivot_row[None, :] == pivot_row[:, None]) & later, axis=1)
    outside = jnp.logical_not(has_later) & (pivot_row >= offset + panel_width)
    spots = jnp.where(outside, pivot_row, full_order)
    ordering = jnp.arange(full_order, dtype=jnp.int32).at[spots].set(before_value, mode="drop")
    return lax.dynamic_update_slice_in_dim(ordering, anchor_value, offset, 0)


def product(left, right):
    return jnp.dot(left, right, precision=lax.Precision.HIGHEST, preferred_element_type=jnp.float32)


def general(matrix, pivots, lower_inv, upper_inv):
    row_blocks, row_part, col_blocks, col_part = matrix.shape
    panel_width = lower_inv.shape[1]
    panel_count = pivots.shape[0]
    full_order = row_blocks * panel_width
    row_devices = lax.axis_size(PROW)
    col_devices = lax.axis_size("pcol")
    row_index = lax.axis_index(PROW)
    col_index = lax.axis_index("pcol")
    local_rows = row_blocks * row_part
    local_cols = col_blocks * col_part
    share_width = local_cols // row_devices
    current = matrix.reshape(local_rows, local_cols)
    global_rows = (
        jnp.arange(row_blocks, dtype=jnp.int32)[:, None] * panel_width
        + row_index * row_part
        + jnp.arange(row_part, dtype=jnp.int32)[None, :]
    ).reshape(local_rows)
    col_span = col_devices * col_part
    global_cols = (
        jnp.arange(col_blocks, dtype=jnp.int32)[:, None] * col_span
        + col_index * col_part
        + jnp.arange(col_part, dtype=jnp.int32)[None, :]
    ).reshape(local_cols)

    def panel(panel_index, current):
        offset = panel_index * panel_width
        ending = offset + panel_width
        ordering = permutation(pivots[panel_index], offset, panel_width, full_order)
        source = ordering[global_rows]
        old_top = lax.dynamic_slice_in_dim(current, panel_index * row_part, row_part, 0)
        old_panel = gathered_by_axis(old_top, PROW, (0, 1), 0)
        wanted = ordering[offset + jnp.arange(panel_width, dtype=jnp.int32)]
        holder = wanted % panel_width // row_part
        local_spot = wanted // panel_width * row_part + wanted % row_part
        picked = jnp.where((holder == row_index)[:, None], current[local_spot], 0.0)
        column_share = sum_by_axis(picked, PROW, 1)
        share_cols = lax.dynamic_slice_in_dim(global_cols, row_index * share_width, share_width)
        solved = product(lower_inv[panel_index], column_share)
        merged = jnp.where((share_cols >= ending)[None, :], solved, column_share)
        top_rows = gathered_by_axis(merged, PROW, (0, 1), 1)
        in_panel = global_rows // panel_width == panel_index
        displaced = (source != global_rows) & jnp.logical_not(in_panel)
        from_old = old_panel[jnp.clip(source - offset, 0, panel_width - 1)]
        current = jnp.where(displaced[:, None], from_old, current)
        own_rows = lax.dynamic_slice_in_dim(top_rows, row_index * row_part, row_part, 0)
        current = lax.dynamic_update_slice_in_dim(current, own_rows, panel_index * row_part, 0)
        trailing_row = global_rows >= ending
        trailing_col = global_cols >= ending
        lower_full = product(current[:, :col_part], upper_inv[panel_index])
        lower_here = jnp.where(trailing_row[:, None], lower_full, 0.0)
        lower_rows = broadcast(lower_here, "pcol", panel_index)
        upper_part = jnp.where(trailing_col[None, :], top_rows, 0.0)
        current = current - product(lower_rows, upper_part)
        own_panel = col_index == panel_index
        new_cols = jnp.where(own_panel & trailing_row[:, None], lower_rows, current[:, :col_part])
        return jnp.concatenate([new_cols, current[:, col_part:]], axis=1)

    current = lax.fori_loop(0, panel_count, panel, current)
    return current.reshape(row_blocks, row_part, col_blocks, col_part)


CLASS_ROWS = 8
MOVED_ROWS = 16


def to_column(row):
    n = row.shape[1]
    eye = lax.broadcasted_iota(jnp.int32, (n, n), 0) == lax.broadcasted_iota(jnp.int32, (n, n), 1)
    return jnp.max(jnp.where(eye, row, -1.0), axis=1, keepdims=True)


def lookup(keys, values, wanted):
    return jnp.max(jnp.where(keys == wanted, values, -1.0), axis=0, keepdims=True)


def find(size, keys, values):
    found = jnp.full((size, 1), -1.0, jnp.float32)
    for key, value in zip(keys, values):
        number = lax.broadcasted_iota(jnp.int32, (size, key.shape[1]), 0).astype(jnp.float32)
        found = jnp.maximum(found, jnp.max(jnp.where(number == key, value, -1.0), axis=1, keepdims=True))
    return found.astype(jnp.int32)


def ranks_of(keys, columns, j, i):
    ranks, smaller = [], []
    for k in range(2):
        rank = jnp.sum(jnp.where((columns[k] == keys[k]) & (j < i), 1.0, 0.0), axis=0, keepdims=True)
        if k == 1:
            rank = rank + jnp.sum(jnp.where(columns[0] == keys[1], 1.0, 0.0), axis=0, keepdims=True)
        ranks.append(rank)
        smaller.append(
            sum(jnp.sum(jnp.where(column < keys[k], 1.0, 0.0), axis=0, keepdims=True) for column in columns)
        )
    return ranks, smaller


def plan_kernel(width, piv_row_ref, pick_ref, fold_ref, perm_ref, pack_ref, place_ref, most_ref):
    me = (lax.axis_index("x") * NZ + lax.axis_index("z")).astype(jnp.float32)
    my_x, my_z = lax.axis_index("x").astype(jnp.float32), lax.axis_index("z").astype(jnp.float32)
    part = width // (NX * NZ)
    j = lax.broadcasted_iota(jnp.int32, (width, width), 0).astype(jnp.float32)
    i = lax.broadcasted_iota(jnp.int32, (width, width), 1).astype(jnp.float32)
    i_row = i[:1]
    sources, spots, spot_cols, befores, before_cols = [], [], [], [], []
    for k in range(2):
        offset = float(k * width)
        p_row = piv_row_ref[k : k + 1, :].astype(jnp.float32)
        p_col = to_column(p_row)
        chain = jnp.max(jnp.where((p_col == offset + i) & (j < i), j, -1.0), axis=0, keepdims=True)
        start = jnp.where(chain >= 0.0, chain, i_row)

        def again(state):
            return state[1] > 0.0

        def jump(state):
            pointer = state[0]
            found = lookup(j[:, :1], to_column(pointer), pointer)
            return found, jnp.max(jnp.abs(found - pointer))

        pointer, _ = lax.while_loop(again, jump, (start, jnp.float32(1.0)))
        before = offset + pointer
        before_col = to_column(before)
        same = p_col == p_row
        last = jnp.max(jnp.where(same & (j < i), j, -1.0), axis=0, keepdims=True)
        later = jnp.max(jnp.where(same & (j > i), 1.0, 0.0), axis=0, keepdims=True)
        anchor = jnp.where(last >= 0.0, lookup(j[:, :1], before_col, last), p_row)
        spot = jnp.where((later == 0.0) & (p_row >= offset + width), p_row, -5.0)
        if k == 1:
            moved = lookup(spot_cols[0], before_cols[0], anchor)
            anchor = jnp.where(moved >= 0.0, moved, anchor)
        sources.append(anchor)
        spots.append(spot)
        spot_cols.append(jnp.max(jnp.where(i == j, spot, -5.0), axis=1, keepdims=True))
        befores.append(before)
        before_cols.append(before_col)

    def divided(value, by):
        return jnp.floor(value * (1.0 / by))

    def holder_and_place(source):
        block = divided(source, width)
        within = source - block * width
        holder = divided(within, part)
        return holder, block * part + within - holder * part

    holders, places = zip(*[holder_and_place(source) for source in sources])
    ranks, smaller = ranks_of(holders, [to_column(h) for h in holders], j, i)
    most = jnp.zeros((1, 1), jnp.float32)
    picks, folds, pick_keys, fold_keys = [], [], [], []
    for k in range(2):
        number = smaller[k] + ranks[k]
        at = divided(number, NZ)
        kind = number - at * NZ
        slot = at - divided(smaller[k] - kind + (NZ - 1.0), NZ)
        most = jnp.maximum(most, jnp.max(slot, axis=1, keepdims=True) - (CLASS_ROWS - 1.0))
        good = slot < CLASS_ROWS
        pick_keys.append(jnp.where((holders[k] == me) & good, kind * CLASS_ROWS + slot, -1.0))
        picks.append(places[k])
        fold_keys.append(jnp.where((kind == my_z) & good, at, -1.0))
        folds.append(holders[k] * CLASS_ROWS + slot)
        perm_ref[k * width : (k + 1) * width, :] = to_column(kind * (2 * width // NZ) + at).astype(jnp.int32)
    pick_ref[...] = find(pick_ref.shape[0], pick_keys, picks)
    fold_ref[...] = find(fold_ref.shape[0], fold_keys, folds)

    landed = lookup(spot_cols[0], before_cols[0], befores[1])
    origins = [befores[0], jnp.where(landed >= 0.0, landed, befores[1])]
    taken = lookup(spot_cols[1], spot_cols[1], spots[0])
    targets = [
        jnp.where((spots[0] >= 2.0 * width) & (taken < 0.0), spots[0], -1.0),
        jnp.where(spots[1] >= 2.0 * width, spots[1], -1.0),
    ]
    owners, rows = zip(*[holder_and_place(origin) for origin in origins])
    ends, spot_rows = zip(*[holder_and_place(jnp.maximum(target, 0.0)) for target in targets])
    owner_x = [divided(owner, NZ) for owner in owners]
    owner_z = [owner - x * NZ for owner, x in zip(owners, owner_x)]
    keys = [
        jnp.where(targets[k] >= 0.0, owner_z[k] * (NX * NZ) + ends[k], 2000.0 + i_row + 600.0 * k) for k in range(2)
    ]
    ranks, _ = ranks_of(keys, [to_column(key) for key in keys], j, i)
    pack_keys, packs, place_keys, place_values = [], [], [], []
    for k in range(2):
        most = jnp.maximum(most, jnp.max(ranks[k], axis=1, keepdims=True) - (MOVED_ROWS - 1.0))
        good = (targets[k] >= 0.0) & (ranks[k] < MOVED_ROWS)
        end_x = divided(ends[k], NZ)
        end_z = ends[k] - end_x * NZ
        pack_keys.append(
            jnp.where(good & (owner_z[k] == my_z) & (end_x == my_x), end_z * MOVED_ROWS + ranks[k], -1.0)
        )
        packs.append(owner_x[k] * (2 * part) + rows[k])
        place_keys.append(jnp.where(good & (ends[k] == me), spot_rows[k], -1.0))
        place_values.append(owner_z[k] * MOVED_ROWS + ranks[k])
    pack_ref[...] = find(pack_ref.shape[0], pack_keys, packs)
    place_ref[...] = find(place_ref.shape[0], place_keys, place_values)
    most_ref[...] = jnp.broadcast_to(most, most_ref.shape).astype(jnp.int32)


def make_plan(pivots, width, rows):
    vmem = pl.BlockSpec(memory_space=pltpu.VMEM)
    sizes = [NZ * CLASS_ROWS, 2 * width // NZ, 2 * width, NZ * MOVED_ROWS, rows]
    shapes = [(n, 1) for n in sizes] + [(8, 128)]
    return pl.pallas_call(
        functools.partial(plan_kernel, width),
        out_shape=[jax.ShapeDtypeStruct(shape, jnp.int32) for shape in shapes],
        in_specs=[vmem],
        out_specs=[vmem] * len(shapes),
        name="row_plan",
    )(pivots)


class Piece:
    def __init__(self, buf, low, high, first, x, z, col, send_sem, recv_sem):
        self.buf, self.low, self.high, self.first = buf, low, high, first
        self.x, self.z, self.col = x, z, col
        self.send_sem, self.recv_sem = send_sem, recv_sem
        self.started = []
        self.na, self.nb = (NX, NZ) if first == "x" else (NZ, NX)
        self.a, self.b = (x, z) if first == "x" else (z, x)

    def place(self, da, db):
        a, b = lax.rem(self.a + da + self.na, self.na), lax.rem(self.b + db + self.nb, self.nb)
        return (a, b) if self.first == "x" else (b, a)

    def copy(self, da, db, to, half, k):
        bx, bz = self.place(da, db)
        middle = (self.low + self.high) // 16 * 8
        low, high = ((self.low, self.high), (self.low, middle), (middle, self.high))[0 if half is None else half + 1]
        view = self.buf.at[bx, bz, low:high]
        return pltpu.make_async_remote_copy(
            src_ref=view,
            dst_ref=view,
            send_sem=self.send_sem.at[bx * NZ + bz, k],
            recv_sem=self.recv_sem.at[bx * NZ + bz, half or 0],
            device_id=self.place(*to) + (self.col,),
            device_id_type=MESH,
        )

    def send(self, da, db, to, half, k):
        copy = self.copy(da, db, to, half, k)
        copy.start()
        self.started.append(copy)

    def receive(self, da, db, half):
        self.copy(da, db, (0, 1), half, 0).wait_recv()

    def along_first(self, d):
        for s in (1, -1):
            if d + 1 <= self.na // 2:
                half = None if d + 1 < self.na // 2 else (1 - s) // 2
                self.send(-s * d, 0, (s, 0), half, (1 - s) // 2)

    def along_second(self, da, d):
        for s in (1, -1):
            if d + 1 <= self.nb // 2:
                half = None if d + 1 < self.nb // 2 else (1 - s) // 2
                self.send(da, -s * d, (0, s), half, (1 - s) // 2 + (2 if d == 0 else 0))

    def first_step(self, d):
        if d == 0:
            self.along_first(0)
            self.along_second(0, 0)
        elif d < self.na // 2:
            for s in (1, -1):
                self.receive(-s * d, 0, None)
            self.along_first(d)
            for s in (1, -1):
                self.along_second(-s * d, 0)
        else:
            self.receive(d, 0, 0)
            self.receive(d, 0, 1)
            self.along_second(d, 0)

    def second_step(self, da, d):
        if d < self.nb // 2:
            for s in (1, -1):
                self.receive(da, -s * d, None)
            self.along_second(da, d)
        else:
            self.receive(da, d, 0)
            self.receive(da, d, 1)

    def steps(self):
        work = [(d, functools.partial(self.first_step, d)) for d in range(self.na // 2 + 1)]
        for d in range(1, self.nb // 2 + 1):
            for ad in range(self.na // 2 + 1):
                for da in [0] if ad == 0 else [ad] if ad == self.na // 2 else [-ad, ad]:
                    work.append((ad + d + 0.5, functools.partial(self.second_step, da, d)))
        return work


class Spread:
    def __init__(self, buf, root, x, z, col, sems):
        self.buf, self.root, self.x, self.z, self.col, self.sems = buf, root, x, z, col, sems
        y, self.core = col // 2, lax.rem(col, 2)
        self.mate = y * 2 + 1 - self.core
        self.up = lax.rem(y + 1, 4) * 2 + self.core
        self.down = lax.rem(y + 3, 4) * 2 + self.core
        self.away = lax.rem(y - root // 2 + 4, 4)

    def copy(self, half, device, k, pair):
        rows = self.buf.shape[0] // 2
        view = self.buf.at[half * rows : (half + 1) * rows]
        return pltpu.make_async_remote_copy(
            src_ref=view,
            dst_ref=view,
            send_sem=self.sems.at[0, half, k],
            recv_sem=self.sems.at[1, half, pair],
            device_id=(self.x, self.z, device),
            device_id_type=MESH,
        )

    def sends(self, hops):
        up = [self.copy(half, self.up, 0, 0) for half in ((0, 1) if hops == 0 else (0,) if hops == 1 else ())]
        down = [self.copy(half, self.down, 1, 0) for half in ((1, 0) if hops == 0 else (1,) if hops == 3 else ())]
        return up, down

    def pass_on(self, half):
        self.copy(half, self.up, 0, 0).wait_recv()
        self.copy(half, self.mate, 2, 1).start()

    def at(self, hops, action):
        pl.when((self.core == self.root % 2) & (self.away == hops))(action)

    def begin(self):
        @pl.when(self.col == self.root)
        def _():
            up, down = self.sends(0)
            for n in range(2):
                up[n].start()
                down[n].start()
                self.copy(n, self.mate, 2, 1).start()

    def relay(self):
        for hops, half in ((1, 0), (3, 1)):

            def action(hops=hops, half=half):
                self.copy(half, self.up, 0, 0).wait_recv()
                for copy in sum(self.sends(hops), []):
                    copy.start()
                self.copy(half, self.mate, 2, 1).start()

            self.at(hops, action)

    def finish(self):
        self.at(1, functools.partial(self.pass_on, 1))
        self.at(3, functools.partial(self.pass_on, 0))

        def both():
            self.pass_on(0)
            self.pass_on(1)

        self.at(2, both)

        @pl.when(self.core != self.root % 2)
        def _():
            for half in range(2):
                self.copy(half, self.mate, 2, 1).wait_recv()

    def close(self):
        for hops in range(4):

            def action(hops=hops):
                for copy in sum(self.sends(hops), []):
                    copy.wait_send()
                for half in range(2):
                    self.copy(half, self.mate, 2, 1).wait_send()

            self.at(hops, action)


def dot(left, right):
    return jnp.dot(left, right, preferred_element_type=jnp.float32)


def split(value):
    high = value.astype(jnp.bfloat16)
    return high, (value - high.astype(jnp.float32)).astype(jnp.bfloat16)


def split_three(value):
    high, rest = split(value)
    low = value - high.astype(jnp.float32) - rest.astype(jnp.float32)
    return high, rest, low.astype(jnp.bfloat16)


def exact(hot, value):
    return sum(dot(hot, term) for term in split_three(value))


def times(left, right):
    return dot(left[0], right[0]) + (dot(left[0], right[1]) + dot(left[1], right[0]))


def hot_of(column, lanes):
    number = lax.broadcasted_iota(jnp.int32, (column.shape[0], lanes), 1)
    return jnp.where(column == number, 1.0, 0.0).astype(jnp.bfloat16)


def blocks(total, step, body):
    def one(n, carry):
        body(pl.multiple_of(n * step, step))
        return carry

    lax.fori_loop(0, total // step, one, 0)


ROWS, BODY, TAIL = 256, 288, 176
LAG, X_ROWS = 3.5, 48


def panels_kernel(
    m_ref, pick_ref, fold_ref, perm_ref, pack_ref, place_ref, linv_ref, uinv_ref, out_ref,
    old, pack_box, place_box, outbox, inbox, g, hot, linv, uinv, t, u, rest, lower0, lower1, low0, low1, solved,
    box_sem, move_sem, old_sem, ring_send, ring_recv, spread_sem0, spread_sem1,
):
    x, z, col = lax.axis_index("x"), lax.axis_index("z"), lax.axis_index("pcol")
    me = x * NZ + z
    count = NX * NZ
    width = linv_ref.shape[1]
    part = width // count
    top = 2 * part
    row_blocks, chunks = m_ref.shape[:2]
    rows, columns = row_blocks * part, chunks * width
    size = 2 * width // NZ
    tail = rows - top
    spread0 = Spread(lower0, 0, x, z, col, spread_sem0)
    spread1 = Spread(lower1, 1, x, z, col, spread_sem1)
    started = []

    others = [lax.rem(me + n, count) for n in range(1, count)]
    barrier = pltpu.get_barrier_semaphore()
    greeted = [(o // NZ, lax.rem(o, NZ), col) for o in others]
    greeted += [(x, z, spread0.mate), (x, z, spread0.up), (x, z, spread0.down)]
    for device in greeted:
        pl.semaphore_signal(barrier, inc=1, device_id=device, device_id_type=MESH)

    for c in range(chunks):
        old[pl.ds(x, 1), :, c * width : (c + 1) * width] = m_ref[0:2, c].reshape(1, top, width)
    pick_hot = hot_of(pick_ref[...], rows)
    tile = width // NX
    for c in range(chunks):
        picked = exact(pick_hot, m_ref[:, c].reshape(rows, width))
        for xs in range(NX):
            outbox[xs * NZ : (xs + 1) * NZ, :, c * tile : (c + 1) * tile] = picked[
                :, xs * tile : (xs + 1) * tile
            ].reshape(NZ, -1, tile)
    inbox[pl.ds(me, 1)] = outbox[pl.ds(me, 1)]
    pl.semaphore_wait(barrier, len(greeted))

    def send(src, dst, send_sem, recv_sem, device):
        copy = pltpu.make_async_remote_copy(
            src_ref=src, dst_ref=dst, send_sem=send_sem, recv_sem=recv_sem, device_id=device, device_id_type=MESH
        )
        copy.start()
        started.append(copy)

    for o in others:
        send(outbox.at[o], inbox.at[me], box_sem.at[0, o], box_sem.at[1, me], (o // NZ, lax.rem(o, NZ), col))
    for d in range(1, NX):
        to = lax.rem(x + d, NX)
        send(old.at[x], old.at[x], old_sem.at[0, to], old_sem.at[1, x], (to, z, col))

    def arrive(view, sem):
        pltpu.make_async_remote_copy(
            src_ref=view, dst_ref=view, send_sem=sem, recv_sem=sem, device_id=(lax.rem(x + 1, NX), z, col),
            device_id_type=MESH,
        ).wait_recv()

    for d in range(1, NX):
        xs = lax.rem(x + d, NX)
        arrive(old.at[xs], old_sem.at[1, xs])
    pack_hot = hot_of(pack_ref[...], NX * top)
    for c in range(0, columns, width):
        packed = exact(pack_hot, old[:, :, c : c + width].reshape(NX * top, width))
        pack_box[:, :, c : c + width] = packed.reshape(NZ, -1, width)
    place_box[pl.ds(z, 1)] = pack_box[pl.ds(z, 1)]
    for o in others:
        arrive(inbox.at[o], box_sem.at[1, o])
    fold_hot = hot_of(fold_ref[...], count * CLASS_ROWS)
    for c in range(chunks):
        mine = exact(fold_hot, inbox[:, :, c * tile : (c + 1) * tile].reshape(count * CLASS_ROWS, tile))
        g[c, pl.ds(x, 1), pl.ds(z, 1)] = mine[None, None]

    pieces, work = [], []
    for c in range(chunks):
        for number, (first, low, high) in enumerate((("x", 0, X_ROWS), ("z", X_ROWS, size))):
            s = 2 * c + number
            pieces.append(Piece(g.at[c], low, high, first, x, z, col, ring_send.at[s], ring_recv.at[s]))
    flow = []
    for number, piece in enumerate(pieces):
        for place, (when, step) in enumerate(piece.steps()):
            flow.append((when + LAG * (number // 2) if when else -1.0, number, place, number // 2, step))
    flow.sort(key=lambda entry: entry[:3])
    for _ in range(2):
        flow.pop(0)[4]()
    for d in range(1, NZ):
        to = lax.rem(z + d, NZ)
        send(pack_box.at[to], place_box.at[z], move_sem.at[0, to], move_sem.at[1, z], (x, to, col))
    for _ in range(2 * chunks - 2):
        flow.pop(0)[4]()

    def prepare():
        for k in range(2):
            linv[k, 0], linv[k, 1] = split(linv_ref[k])
            uinv[k, 0], uinv[k, 1] = split(uinv_ref[k])

        def perm(r):
            hot[pl.ds(r, 128)] = hot_of(perm_ref[pl.ds(r, 128), :], 2 * width)

        blocks(2 * width, 128, perm)

    def place_moved():
        for d in range(1, NZ):
            zs = lax.rem(z + d, NZ)
            arrive(place_box.at[zs], move_sem.at[1, zs])
        column = place_ref[...]
        place_hot = hot_of(column[top:], NZ * MOVED_ROWS)
        for c in range(chunks):
            cols = slice(c * width, (c + 1) * width)
            moved = exact(place_hot, place_box[:, :, cols].reshape(NZ * MOVED_ROWS, width))
            rest[width:, cols] = jnp.where(column[top:] >= 0, moved, m_ref[2:, c].reshape(tail, width))

    def permute(c):
        whole = jnp.concatenate([g[c, n].reshape(2 * width, tile) for n in range(NX)], axis=1)
        high, middle = split(whole)

        def body(r):
            left = hot[pl.ds(r, ROWS)]
            first, second = dot(left, high), dot(left, middle)
            t[0, pl.ds(r, ROWS)] = first.astype(jnp.bfloat16)
            t[1, pl.ds(r, ROWS)] = second.astype(jnp.bfloat16)

            @pl.when(r >= width)
            def _():
                rest[pl.ds(r - width, ROWS), c * width : (c + 1) * width] = first + second

        blocks(2 * width, ROWS, body)

    def own(ref):
        return ref[pl.ds(pl.multiple_of(me * part, part), part)]

    def solve0(c):
        right = t[0, 0:width], t[1, 0:width]
        cols = slice(c * width, (c + 1) * width)

        def body(r):
            value = times((linv[0, 0, pl.ds(r, ROWS)], linv[0, 1, pl.ds(r, ROWS)]), right)
            u[0, 0, pl.ds(r, ROWS), cols], u[0, 1, pl.ds(r, ROWS), cols] = split(value)
            solved[pl.ds(r, ROWS)] = value

        blocks(width, ROWS, body)
        out_ref[0, c] = own(solved)
        if c == 0:

            @pl.when(col == 0)
            def _():
                out_ref[0, c] = own(t.at[0]).astype(jnp.float32) + own(t.at[1]).astype(jnp.float32)
                u[0, :, :, cols] = jnp.zeros((2, width, width), jnp.bfloat16)

    def find_lower0():
        @pl.when(col == 0)
        def _():
            right = uinv[0, 0], uinv[0, 1]

            def body(r):
                lower0[pl.ds(r, BODY)] = times(split(rest[pl.ds(r, BODY), 0:width]), right)

            blocks(width + tail, BODY, body)

    def split_lower(source, target):
        def body(r):
            target[0, pl.ds(r, 32)], target[1, pl.ds(r, 32)] = split(source[pl.ds(r, 32)])

        blocks(source.shape[0], 32, body)

    def reduce0(c):
        cols = slice(c * width, (c + 1) * width)
        right = u[0, 0, :, cols], u[0, 1, :, cols]

        def body(r):
            rest[pl.ds(r, BODY), cols] -= times((low0[0, pl.ds(r, BODY)], low0[1, pl.ds(r, BODY)]), right)

        blocks(width + tail, BODY, body)

    def find_lower1():
        right = uinv[1, 0], uinv[1, 1]

        def body(r):
            lower1[pl.ds(r, TAIL)] = times(split(rest[pl.ds(width + r, TAIL), 0:width]), right)

        blocks(tail, TAIL, body)

    def solve1(c):
        cols = slice(c * width, (c + 1) * width)
        right = split(rest[0:width, cols])

        def body(r):
            value = times((linv[1, 0, pl.ds(r, ROWS)], linv[1, 1, pl.ds(r, ROWS)]), right)
            u[1, 0, pl.ds(r, ROWS), cols], u[1, 1, pl.ds(r, ROWS), cols] = split(value)
            solved[pl.ds(r, ROWS)] = value

        blocks(width, ROWS, body)
        out_ref[1, c] = own(solved)
        if c == 0:

            @pl.when(col <= 1)
            def _():
                mine = jnp.where(col == 0, own(lower0), rest[pl.ds(pl.multiple_of(me * part, part), part), cols])
                out_ref[1, c] = mine
                u[1, :, :, cols] = jnp.zeros((2, width, width), jnp.bfloat16)

    def reduce1(c):
        cols = slice(c * width, (c + 1) * width)
        right = u[1, 0, :, cols], u[1, 1, :, cols]

        def body(r):
            value = rest[pl.ds(width + r, TAIL), cols] - times((low1[0, pl.ds(r, TAIL)], low1[1, pl.ds(r, TAIL)]), right)
            if c == 0:
                value = jnp.where(col == 0, lower0[pl.ds(width + r, TAIL)], jnp.where(col == 1, lower1[pl.ds(r, TAIL)], value))
            out_ref[pl.ds(2 + r // part, TAIL // part), c] = value.reshape(TAIL // part, part, width)

        blocks(tail, TAIL, body)

    def left_of(stage):
        return max([n + 1 for n, entry in enumerate(flow) if entry[3] <= stage], default=0)

    def mix(stage, actions):
        total = left_of(stage)
        done = 0
        for number, action in enumerate(actions):
            until = (number + 1) * total // (len(actions) + 1)
            for _ in range(until - done):
                flow.pop(0)[4]()
            done = until
            action()
        for _ in range(total - done):
            flow.pop(0)[4]()

    P_ = functools.partial
    def lower_arrives():
        spread0.finish()
        split_lower(lower0, low0)
        reduce0(0)

    def early():
        @pl.when(col == 1)
        def _():
            lower_arrives()
            find_lower1()

        spread1.begin()

    def late():
        pl.when(col != 1)(lower_arrives)

    mix(0, [prepare])
    place_moved()
    permute(0)
    find_lower0()
    spread0.begin()
    solve0(0)
    early()
    mix(1, [spread0.relay])
    mix(2, [P_(permute, 1), P_(solve0, 1), late, spread1.relay, P_(reduce0, 1), P_(solve1, 0)])
    permute(2)
    solve0(2)
    reduce0(2)
    solve1(1)
    solve1(2)
    spread1.finish()
    split_lower(lower1, low1)
    for c in range(chunks):
        reduce1(c)
    for copy in started:
        copy.wait_send()
    for piece in pieces:
        for copy in piece.started:
            copy.wait_send()
    spread0.close()
    spread1.close()


def two_panels(matrix, plan, lower_inv, upper_inv):
    row_blocks, part, chunks, width = matrix.shape
    rows, columns = row_blocks * part, chunks * width
    count, top, size, tile = NX * NZ, 2 * width // (NX * NZ), 2 * width // NZ, width // NX
    tail = rows - top
    vmem = pl.BlockSpec(memory_space=pltpu.VMEM)
    f32, bf16, dma = jnp.float32, jnp.bfloat16, pltpu.SemaphoreType.DMA
    result = pl.pallas_call(
        panels_kernel,
        out_shape=jax.ShapeDtypeStruct((row_blocks, chunks, part, width), f32),
        in_specs=[vmem] * 8,
        out_specs=vmem,
        scratch_shapes=[
            pltpu.VMEM((NX, top, columns), f32),
            pltpu.VMEM((NZ, MOVED_ROWS, columns), f32),
            pltpu.VMEM((NZ, MOVED_ROWS, columns), f32),
            pltpu.VMEM((count, CLASS_ROWS, columns // NX), f32),
            pltpu.VMEM((count, CLASS_ROWS, columns // NX), f32),
            pltpu.VMEM((chunks, NX, NZ, size, tile), f32),
            pltpu.VMEM((2 * width, 2 * width), bf16),
            pltpu.VMEM((2, 2, width, width), bf16),
            pltpu.VMEM((2, 2, width, width), bf16),
            pltpu.VMEM((2, 2 * width, width), bf16),
            pltpu.VMEM((2, 2, width, columns), bf16),
            pltpu.VMEM((width + tail, columns), f32),
            pltpu.VMEM((width + tail, width), f32),
            pltpu.VMEM((tail, width), f32),
            pltpu.VMEM((2, width + tail, width), bf16),
            pltpu.VMEM((2, tail, width), bf16),
            pltpu.VMEM((width, width), f32),
            dma((2, count)),
            dma((2, NZ)),
            dma((2, NX)),
            dma((2 * chunks, count, 4)),
            dma((2 * chunks, count, 2)),
            dma((2, 2, 3)),
            dma((2, 2, 3)),
        ],
        compiler_params=pltpu.CompilerParams(
            collective_id=0, has_side_effects=True, vmem_limit_bytes=62 * 2**20
        ),
        name="two_panels",
    )(matrix.transpose(0, 2, 1, 3), *plan, lower_inv, upper_inv)
    return result.transpose(0, 2, 1, 3)


def local(matrix, pivots, lower_inv, upper_inv):
    row_blocks, row_part, col_blocks, col_part = matrix.shape
    width = lower_inv.shape[1]
    *plan, most = make_plan(pivots, width, row_blocks * row_part)
    return lax.cond(
        most[0, 0] <= 0,
        lambda m, p, a, b, q: two_panels(m, q, a, b),
        lambda m, p, a, b, q: general(m, p, a, b),
        matrix, pivots, lower_inv, upper_inv, plan,
    )


def solution(mesh):
    finer = Mesh(mesh.devices.reshape(NX, NZ, mesh.shape["pcol"]), ("x", "z", "pcol"))
    in_specs = (P(None, PROW, None, "pcol"), P(), P(), P())
    out_specs = P(None, PROW, None, "pcol")
    return jax.shard_map(local, mesh=finer, in_specs=in_specs, out_specs=out_specs, check_vma=False)
```

profile of v0, /device:TPU:8, one launch (start us, length us, event | category | flops | bytes accessed | tf_op | source)
XLA Modules:
  0.0 165.6 jit_solution(17755297786367833992)
XLA Ops:
  6.5 5.5 %row_plan.1 = (s32[64,1]{1,0:T(8,128)S(1)}, s32[128,1]{1,0:T(8,128)S(1)}, s32[1024,1]{1,0:T(8,128)}, s32[128,1]{1,0:T(8,128)}, s32[384,1]{1,0:T(8,128)S(1)}, /*index=5*/s32[8,128]{1,0:T(8,128)}) custom-call(s32[2,512]{1,0:T(2,128)} %piv_row_ref.1), custom_call_target="tpu_custom_call" | custom-call | tf_op jit(solution)/shard_map/row_plan/pallas_call | solution.py:274
  12.0 1.3 slice.36
  13.9 141.4 %conditional.1 = (f32[24,16,3,512]{3,1,2,0:T(8,128)}) conditional(s32[]{:T(128)} %bitcast.2, (f32[24,16,3,512]{3,1,2,0:T(8,128)}, s32[2,512]{1,0:T(2,128)}, f32[2,512,512]{2,1,0:T(8,128)}, f32[2,512,512]{2,1,0:T(8,128)}) %tuple.36, (f32[24,16,3,512]{3,1,2,0:T(8,128)}, s32[64,1]{1,0:T(8,128)S(1)}, s32[128,1]{1,0:T(8,128)S(1)}, s32[1024,1]{1,0:T(8,128)}, ...), branch_computations={%region_0.9_spmd, %region_9.10_spmd} | conditional | flops 4990086656 | bytes 151163360 | solution.py:805
  14.1 141.0 %two_panels.1 = f32[24,3,16,512]{3,2,1,0:T(8,128)} custom-call(f32[24,3,16,512]{3,2,1,0:T(8,128)} %bitcast.176, s32[64,1]{1,0:T(8,128)S(1)} %get-tuple-element.355.pick_ref, s32[128,1]{1,0:T(8,128)S(1)} %get-tuple-element.356.fold_ref, s32[1024,1]{1,0:T(8,128)} %get-tuple-element.357.perm_ref, s32[128,1]{1,0:T(8,128)} %get-tuple-element.358.pack_ref, ...), custom_call_target="tpu_custom_call" | custom-call | tf_op jit(solution)/shard_map/cond/branch_1_fun/two_panels/pallas_call | solution.py:762
  155.4 3.4 %copy.64 = f32[24,16,3,512]{3,1,2,0:T(8,128)} copy(f32[24,16,3,512]{3,1,2,0:T(8,128)} %get-tuple-element.458) | data formatting | bytes 4718592
where the time goes:
time: 166 us
  Pallas kernels  147 us (89%)
  between operations  14 us (8%)
  local copies, waits for them, and re-layouts  4.7 us (3%)
    pallas_call x1, Pallas kernels, two_panels(): pl.pallas_call(panels_kernel, out_shape=jax.ShapeDtypeStruct((row_blocks,...  141 us
    pallas_call x1, Pallas kernels, make_plan(): pl.pallas_call(functools.partial(plan_kernel, width), out_shape=[jax.Shap...  5.51 us
    unnamed x1, local copies, waits for them, and re-layouts  3.44 us

commit v1 on v0

--- a/solution.py
+++ b/solution.py
@@ -19,28 +19,36 @@
     return jnp.moveaxis(parts, 0, dim).reshape(shape)
 
 
-def all_blocks(x, axes, order):
-    parts = x
-    for k in order:
-        parts = lax.all_gather(parts, axes[k])
-    done = order[::-1]
-    back = [done.index(k) for k in range(len(axes))]
-    parts = parts.transpose(*back, *range(len(axes), parts.ndim))
-    return parts.reshape(-1, *x.shape)
-
-
-def gathered_by_axis(x, axes, order, dim):
-    return in_order(all_blocks(x, axes, order), dim)
-
-
-def sum_by_axis(x, axes, dim):
-    for axis in axes:
-        x = lax.psum_scatter(x, axis, scatter_dimension=dim, tiled=True)
-    return x
+def to_next(x, axis):
+    size = lax.axis_size(axis)
+    return lax.ppermute(x, axis, [(n, (n + 1) % size) for n in range(size)])
+
+
+def gathered_by_axis(x, axis, dim):
+    size, me = lax.axis_size(axis), lax.axis_index(axis)
+
+    def turn(n, state):
+        parts, block = state
+        block = to_next(block, axis)
+        return lax.dynamic_update_index_in_dim(parts, block, (me - n + size) % size, 0), block
+
+    parts = lax.dynamic_update_index_in_dim(jnp.zeros((size, *x.shape), x.dtype), x, me, 0)
+    return in_order(lax.fori_loop(1, size, turn, (parts, x))[0], dim)
+
+
+def sum_by_axis(x, axis, dim):
+    size, me = lax.axis_size(axis), lax.axis_index(axis)
+    width = x.shape[dim] // size
+
+    def term(n):
+        return lax.dynamic_slice_in_dim(x, (me - 1 - n + size) % size * width, width, dim)
+
+    return lax.fori_loop(1, size, lambda n, total: to_next(total, axis) + term(n), term(0))
 
 
 def broadcast(x, axis, root):
-    return lax.dynamic_index_in_dim(lax.all_gather(x, axis), root, 0, keepdims=False)
+    mine = lax.axis_index(axis) == root
+    return lax.fori_loop(1, lax.axis_size(axis), lambda n, y: jnp.where(mine, x, to_next(y, axis)), x)
 
 
 def permutation(pivot_row, offset, panel_width, full_order):
@@ -101,7 +109,7 @@
         ordering = permutation(pivots[panel_index], offset, panel_width, full_order)
         source = ordering[global_rows]
         old_top = lax.dynamic_slice_in_dim(current, panel_index * row_part, row_part, 0)
-        old_panel = gathered_by_axis(old_top, PROW, (0, 1), 0)
+        old_panel = gathered_by_axis(old_top, PROW, 0)
         wanted = ordering[offset + jnp.arange(panel_width, dtype=jnp.int32)]
         holder = wanted % panel_width // row_part
         local_spot = wanted // panel_width * row_part + wanted % row_part
@@ -110,7 +118,7 @@
         share_cols = lax.dynamic_slice_in_dim(global_cols, row_index * share_width, share_width)
         solved = product(lower_inv[panel_index], column_share)
         merged = jnp.where((share_cols >= ending)[None, :], solved, column_share)
-        top_rows = gathered_by_axis(merged, PROW, (0, 1), 1)
+        top_rows = gathered_by_axis(merged, PROW, 1)
         in_panel = global_rows // panel_width == panel_index
         displaced = (source != global_rows) & jnp.logical_not(in_panel)
         from_old = old_panel[jnp.clip(source - offset, 0, panel_width - 1)]
@@ -360,6 +368,23 @@
         return work
 
 
+class Several:
+    def __init__(self, copies):
+        self.copies = copies
+
+    def start(self):
+        for copy in self.copies:
+            copy.start()
+
+    def wait_send(self):
+        for copy in self.copies:
+            copy.wait_send()
+
+    def wait_recv(self):
+        for copy in self.copies:
+            copy.wait_recv()
+
+
 class Spread:
     def __init__(self, buf, root, x, z, col, sems):
         self.buf, self.root, self.x, self.z, self.col, self.sems = buf, root, x, z, col, sems
@@ -370,13 +395,19 @@
         self.away = lax.rem(y - root // 2 + 4, 4)
 
     def copy(self, half, device, k, pair):
-        rows = self.buf.shape[0] // 2
-        view = self.buf.at[half * rows : (half + 1) * rows]
+        return Several([self.one(half, n, device, k, pair) for n in range(QUARTERS)])
+
+    def one(self, half, n, device, k, pair):
+        rows = self.buf.shape[0] // 16 * 8
+        low = half * rows
+        high = self.buf.shape[0] if half else rows
+        cut = [low + (high - low) * m // (8 * QUARTERS) * 8 for m in range(QUARTERS)] + [high]
+        view = self.buf.at[cut[n] : cut[n + 1]]
         return pltpu.make_async_remote_copy(
             src_ref=view,
             dst_ref=view,
-            send_sem=self.sems.at[0, half, k],
-            recv_sem=self.sems.at[1, half, pair],
+            send_sem=self.sems.at[0, half, k, n],
+            recv_sem=self.sems.at[1, half, pair, n],
             device_id=(self.x, self.z, device),
             device_id_type=MESH,
         )
@@ -478,6 +509,7 @@
 
 ROWS, BODY, TAIL = 256, 288, 176
 LAG, X_ROWS = 3.5, 48
+QUARTERS = 1
 
 
 def panels_kernel(
@@ -787,8 +819,8 @@
             dma((2, NX)),
             dma((2 * chunks, count, 4)),
             dma((2 * chunks, count, 2)),
-            dma((2, 2, 3)),
-            dma((2, 2, 3)),
+            dma((2, 2, 3, QUARTERS)),
+            dma((2, 2, 3, QUARTERS)),
         ],
         compiler_params=pltpu.CompilerParams(
             collective_id=0, has_side_effects=True, vmem_limit_bytes=62 * 2**20

time: 166 us -> 153 us (0.922)
  between operations: 14 us -> 0.65 us
where the time goes in v1:
time: 153 us
  Pallas kernels  147 us (96%)
  local copies, waits for them, and re-layouts  4.7 us (3%)
    pallas_call x1, Pallas kernels, two_panels(): pl.pallas_call(panels_kernel, out_shape=jax.ShapeDtypeStruct((row_blocks,...  141 us
    pallas_call x1, Pallas kernels, make_plan(): pl.pallas_call(functools.partial(plan_kernel, width), out_shape=[jax.Shap...  5.74 us
    unnamed x1, local copies, waits for them, and re-layouts  3.44 us

profile of v1, /device:TPU:8, one launch (start us, length us, event | category | flops | bytes accessed | tf_op | source)
XLA Modules:
  0.0 152.6 jit_solution(13016629127370412950)
XLA Ops:
  0.0 5.7 %row_plan.1 = (s32[64,1]{1,0:T(8,128)}, s32[128,1]{1,0:T(8,128)S(1)}, s32[1024,1]{1,0:T(8,128)}, s32[128,1]{1,0:T(8,128)S(1)}, s32[384,1]{1,0:T(8,128)}, /*index=5*/s32[8,128]{1,0:T(8,128)}) custom-call(s32[2,512]{1,0:T(2,128)} %piv_row_ref.1), custom_call_target="tpu_custom_call" | custom-call | tf_op jit(solution)/shard_map/row_plan/pallas_call | solution.py:282
  5.7 1.3 slice.45
  7.6 141.5 %conditional.1 = (f32[24,16,3,512]{3,1,2,0:T(8,128)}) conditional(s32[]{:T(128)} %bitcast.4, (f32[24,16,3,512]{3,1,2,0:T(8,128)}, s32[2,512]{1,0:T(2,128)}, f32[2,512,512]{2,1,0:T(8,128)}, f32[2,512,512]{2,1,0:T(8,128)}) %tuple.126, (f32[24,16,3,512]{3,1,2,0:T(8,128)}, s32[64,1]{1,0:T(8,128)}, s32[128,1]{1,0:T(8,128)S(1)}, s32[1024,1]{1,0:T(8,128)}, ...), branch_computations={%region_0.15_spmd, %region_15.16_spmd} | conditional | flops 4990307840 | bytes 96702216 | solution.py:837
  7.8 141.1 %two_panels.1 = f32[24,3,16,512]{3,2,1,0:T(8,128)} custom-call(f32[24,3,16,512]{3,2,1,0:T(8,128)} %bitcast.143, s32[64,1]{1,0:T(8,128)} %get-tuple-element.838.pick_ref, s32[128,1]{1,0:T(8,128)S(1)} %get-tuple-element.839.fold_ref, s32[1024,1]{1,0:T(8,128)} %get-tuple-element.840.perm_ref, s32[128,1]{1,0:T(8,128)S(1)} %get-tuple-element.841.pack_ref, ...), custom_call_target="tpu_custom_call" | custom-call | tf_op jit(solution)/shard_map/cond/branch_1_fun/two_panels/pallas_call | solution.py:794
  149.1 3.4 %copy.93 = f32[24,16,3,512]{3,1,2,0:T(8,128)} copy(f32[24,16,3,512]{3,1,2,0:T(8,128)} %get-tuple-element.956) | data formatting | bytes 4718592

commit v2 on v1

--- a/solution.py
+++ b/solution.py
@@ -278,7 +278,7 @@
 def make_plan(pivots, width, rows):
     vmem = pl.BlockSpec(memory_space=pltpu.VMEM)
     sizes = [NZ * CLASS_ROWS, 2 * width // NZ, 2 * width, NZ * MOVED_ROWS, rows]
-    shapes = [(n, 1) for n in sizes] + [(8, 128)]
+    shapes = [(n, 1) for n in sizes] + [(1, 1)]
     return pl.pallas_call(
         functools.partial(plan_kernel, width),
         out_shape=[jax.ShapeDtypeStruct(shape, jnp.int32) for shape in shapes],
@@ -757,8 +757,7 @@
     def late():
         pl.when(col != 1)(lower_arrives)
 
-    mix(0, [prepare])
-    place_moved()
+    mix(0, [prepare, place_moved])
     permute(0)
     find_lower0()
     spread0.begin()

time: 153 us -> 150 us (0.980)
  Pallas kernels: 147 us -> 145 us
    pallas_call x1, Pallas kernels: 141 us -> 139 us  [two_panels(): pl.pallas_call(panels_kernel, out_shape=jax.ShapeDtypeStruct((row_blocks,...]
where the time goes in v2:
time: 150 us
  Pallas kernels  145 us (97%)
  local copies, waits for them, and re-layouts  3.44 us (2%)
    pallas_call x1, Pallas kernels, two_panels(): pl.pallas_call(panels_kernel, out_shape=jax.ShapeDtypeStruct((row_blocks,...  139 us
    pallas_call x1, Pallas kernels, make_plan(): pl.pallas_call(functools.partial(plan_kernel, width), out_shape=[jax.Shap...  5.74 us
    unnamed x1, local copies, waits for them, and re-layouts  3.44 us

profile of v2, /device:TPU:8, one launch (start us, length us, event | category | flops | bytes accessed | tf_op | source)
XLA Modules:
  0.0 149.6 jit_solution(10248988628453811755)
XLA Ops:
  0.0 5.7 %row_plan.1 = (s32[64,1]{1,0:T(8,128)}, s32[128,1]{1,0:T(8,128)S(1)}, s32[1024,1]{1,0:T(8,128)}, s32[128,1]{1,0:T(8,128)S(1)}, s32[384,1]{1,0:T(8,128)}, /*index=5*/s32[1,1]{1,0:T(1,128)}) custom-call(s32[2,512]{1,0:T(2,128)} %piv_row_ref.1), custom_call_target="tpu_custom_call" | custom-call | tf_op jit(solution)/shard_map/row_plan/pallas_call | solution.py:282
  6.4 139.8 %conditional.1 = (f32[24,16,3,512]{3,1,2,0:T(8,128)}) conditional(s32[]{:T(128)} %bitcast.4, (f32[24,16,3,512]{3,1,2,0:T(8,128)}, s32[2,512]{1,0:T(2,128)}, f32[2,512,512]{2,1,0:T(8,128)}, f32[2,512,512]{2,1,0:T(8,128)}) %tuple.126, (f32[24,16,3,512]{3,1,2,0:T(8,128)}, s32[64,1]{1,0:T(8,128)}, s32[128,1]{1,0:T(8,128)S(1)}, s32[1024,1]{1,0:T(8,128)}, ...), branch_computations={%region_0.15_spmd, %region_15.16_spmd} | conditional | flops 4990307840 | bytes 96702216 | solution.py:836
  6.6 139.4 %two_panels.1 = f32[24,3,16,512]{3,2,1,0:T(8,128)} custom-call(f32[24,3,16,512]{3,2,1,0:T(8,128)} %bitcast.143, s32[64,1]{1,0:T(8,128)} %get-tuple-element.838.pick_ref, s32[128,1]{1,0:T(8,128)S(1)} %get-tuple-element.839.fold_ref, s32[1024,1]{1,0:T(8,128)} %get-tuple-element.840.perm_ref, s32[128,1]{1,0:T(8,128)S(1)} %get-tuple-element.841.pack_ref, ...), custom_call_target="tpu_custom_call" | custom-call | tf_op jit(solution)/shard_map/cond/branch_1_fun/two_panels/pallas_call | solution.py:793
  146.2 3.4 %copy.93 = f32[24,16,3,512]{3,1,2,0:T(8,128)} copy(f32[24,16,3,512]{3,1,2,0:T(8,128)} %get-tuple-element.956) | data formatting | bytes 4718592

commit v3 on v2

--- a/solution.py
+++ b/solution.py
@@ -429,9 +429,9 @@
         def _():
             up, down = self.sends(0)
             for n in range(2):
+                self.copy(n, self.mate, 2, 1).start()
                 up[n].start()
                 down[n].start()
-                self.copy(n, self.mate, 2, 1).start()
 
     def relay(self):
         for hops, half in ((1, 0), (3, 1)):
@@ -624,11 +624,12 @@
             moved = exact(place_hot, place_box[:, :, cols].reshape(NZ * MOVED_ROWS, width))
             rest[width:, cols] = jnp.where(column[top:] >= 0, moved, m_ref[2:, c].reshape(tail, width))
 
-    def permute(c):
+    def permute(c, begin=0, end=2 * width):
         whole = jnp.concatenate([g[c, n].reshape(2 * width, tile) for n in range(NX)], axis=1)
         high, middle = split(whole)
 
-        def body(r):
+        def body(n):
+            r = pl.multiple_of(begin + n, ROWS)
             left = hot[pl.ds(r, ROWS)]
             first, second = dot(left, high), dot(left, middle)
             t[0, pl.ds(r, ROWS)] = first.astype(jnp.bfloat16)
@@ -638,7 +639,7 @@
             def _():
                 rest[pl.ds(r - width, ROWS), c * width : (c + 1) * width] = first + second
 
-        blocks(2 * width, ROWS, body)
+        blocks(end - begin, ROWS, body)
 
     def own(ref):
         return ref[pl.ds(pl.multiple_of(me * part, part), part)]
@@ -758,9 +759,10 @@
         pl.when(col != 1)(lower_arrives)
 
     mix(0, [prepare, place_moved])
-    permute(0)
+    permute(0, width, 2 * width)
     find_lower0()
     spread0.begin()
+    permute(0, 0, width)
     solve0(0)
     early()
     mix(1, [spread0.relay])

time: 150 us -> 148 us (0.987)
  no operation moved by 1% of the time
where the time goes in v3:
time: 148 us
  Pallas kernels  144 us (97%)
  local copies, waits for them, and re-layouts  3.44 us (2%)
    pallas_call x1, Pallas kernels, two_panels(): pl.pallas_call(panels_kernel, out_shape=jax.ShapeDtypeStruct((row_blocks,...  138 us
    pallas_call x1, Pallas kernels, make_plan(): pl.pallas_call(functools.partial(plan_kernel, width), out_shape=[jax.Shap...  5.74 us
    unnamed x1, local copies, waits for them, and re-layouts  3.44 us

profile of v3, /device:TPU:8, one launch (start us, length us, event | category | flops | bytes accessed | tf_op | source)
XLA Modules:
  0.0 148.2 jit_solution(17739337984960328160)
XLA Ops:
  0.0 5.7 %row_plan.1 = (s32[64,1]{1,0:T(8,128)}, s32[128,1]{1,0:T(8,128)S(1)}, s32[1024,1]{1,0:T(8,128)}, s32[128,1]{1,0:T(8,128)S(1)}, s32[384,1]{1,0:T(8,128)}, /*index=5*/s32[1,1]{1,0:T(1,128)}) custom-call(s32[2,512]{1,0:T(2,128)} %piv_row_ref.1), custom_call_target="tpu_custom_call" | custom-call | tf_op jit(solution)/shard_map/row_plan/pallas_call | solution.py:282
  6.4 138.3 %conditional.1 = (f32[24,16,3,512]{3,1,2,0:T(8,128)}) conditional(s32[]{:T(128)} %bitcast.4, (f32[24,16,3,512]{3,1,2,0:T(8,128)}, s32[2,512]{1,0:T(2,128)}, f32[2,512,512]{2,1,0:T(8,128)}, f32[2,512,512]{2,1,0:T(8,128)}) %tuple.126, (f32[24,16,3,512]{3,1,2,0:T(8,128)}, s32[64,1]{1,0:T(8,128)}, s32[128,1]{1,0:T(8,128)S(1)}, s32[1024,1]{1,0:T(8,128)}, ...), branch_computations={%region_0.15_spmd, %region_15.16_spmd} | conditional | flops 4990307840 | bytes 96702216 | solution.py:838
  6.6 138.0 %two_panels.1 = f32[24,3,16,512]{3,2,1,0:T(8,128)} custom-call(f32[24,3,16,512]{3,2,1,0:T(8,128)} %bitcast.143, s32[64,1]{1,0:T(8,128)} %get-tuple-element.838.pick_ref, s32[128,1]{1,0:T(8,128)S(1)} %get-tuple-element.839.fold_ref, s32[1024,1]{1,0:T(8,128)} %get-tuple-element.840.perm_ref, s32[128,1]{1,0:T(8,128)S(1)} %get-tuple-element.841.pack_ref, ...), custom_call_target="tpu_custom_call" | custom-call | tf_op jit(solution)/shard_map/cond/branch_1_fun/two_panels/pallas_call | solution.py:795
  144.7 3.4 %copy.93 = f32[24,16,3,512]{3,1,2,0:T(8,128)} copy(f32[24,16,3,512]{3,1,2,0:T(8,128)} %get-tuple-element.956) | data formatting | bytes 4718592
